TPU v7x, 512 devices: a whole 4x4x16 slice. The times are simulated.
512 devices in a mesh: space: 16 (over y, x_hi, core), energy: 32 (over z, x_lo).
Axes of the slice: x: 4 (x_hi: 2, x_lo: 2; x = x_hi * 2 + x_lo), y: 4, z: 16, core: 2. Of those that a mesh axis runs over, the one named last changes fastest.
Arguments:
- lesser: bfloat16 [32, 16, 3, 128, 256], P('energy', 'space'), may hold values from -6 to 6
- greater: bfloat16 [32, 16, 3, 128, 256], P('energy', 'space'), may hold values from -1.0546875 to 1.0546875
Outputs:
- polarization: float32 [32, 16, 3, 128, 256], P('energy', 'space')
All inputs are finite; a program needn't handle non-finite values.
Results may differ from a plain program's by a relative error of at most 0.0003.
Values may be sent and summed in bfloat16 or wider, within the bound.
A program may use at most 64 MiB of HBM per device.

v0:
```python
import math

import jax
import jax.numpy as jnp
from jax import lax
from jax.sharding import PartitionSpec as P


def with_halo(block, sides, width):
    for axis, dim in sides:
        count = lax.axis_size(axis)
        forward = [(i, i + 1) for i in range(count - 1)]
        backward = [(target, source) for source, target in forward]
        low = lax.ppermute(
            lax.slice_in_dim(block, block.shape[dim] - width, None, axis=dim), axis, forward
        )
        high = lax.ppermute(lax.slice_in_dim(block, 0, width, axis=dim), axis, backward)
        block = jnp.concatenate([low, block, high], axis=dim)
    return block


def flip_tiles(tiles):
    shape = tiles.shape
    width = shape[-2]
    split = tiles.reshape(shape[:-1] + (2, width))
    turned = jnp.swapaxes(split, -3, -1)
    return turned.reshape(shape)


def correlate_rows(pair):
    left, right = pair
    total = left.shape[0]
    inner = left.shape[1:-1]
    width = left.shape[-1] // 2
    left = left.astype(jnp.float32).reshape((total, -1, 2, width))
    right = right.astype(jnp.float32).reshape((total, -1, 2, width))
    left_re = left[:, :, 0].reshape((total, -1))
    left_im = left[:, :, 1].reshape((total, -1))
    right_re = right[:, :, 0].reshape((total, -1))
    right_im = right[:, :, 1].reshape((total, -1))
    freq = lax.broadcasted_iota(jnp.int32, (total, total), 0)
    point = lax.broadcasted_iota(jnp.int32, (total, total), 1)
    phase = (freq * point % total).astype(jnp.float32) * (2.0 * math.pi / total)
    cosine = jnp.cos(phase)
    sine = jnp.sin(phase)
    high = lax.Precision.HIGHEST

    def apply(matrix, data):
        return jnp.dot(matrix, data, precision=high, preferred_element_type=jnp.float32)

    lhat_re = apply(cosine, left_re) + apply(sine, left_im)
    lhat_im = apply(cosine, left_im) - apply(sine, left_re)
    ghat_re = apply(cosine, right_re) - apply(sine, right_im)
    ghat_im = apply(cosine, right_im) + apply(sine, right_re)
    prod_re = lhat_re * ghat_re - lhat_im * ghat_im
    prod_im = lhat_re * ghat_im + lhat_im * ghat_re
    out_re = (apply(cosine.T, prod_re) - apply(sine.T, prod_im)) / total
    out_im = (apply(cosine.T, prod_im) + apply(sine.T, prod_re)) / total
    result = jnp.concatenate(
        [out_re.reshape((total,) + inner + (width,)), out_im.reshape((total,) + inner + (width,))],
        axis=-1,
    )
    return lax.all_to_all(result, "energy", split_axis=0, concat_axis=2, tiled=True)


def on_device(lesser, greater):
    own_lesser = lesser[:, 0]
    own_greater = greater[:, 0]
    rims = jnp.stack([own_greater[:, 0], own_greater[:, 2]], axis=1)
    padded = with_halo(rims, (("space", 1),), 1)
    mirrored = flip_tiles(jnp.stack([padded[:, 0], own_greater[:, 1], padded[:, 3]], axis=1))
    summed = correlate_rows(
        (
            lax.all_to_all(own_lesser, "energy", split_axis=2, concat_axis=0, tiled=True),
            lax.all_to_all(mirrored, "energy", split_axis=2, concat_axis=0, tiled=True),
        )
    )
    return summed[:, None]


def solution(mesh):
    return jax.shard_map(
        on_device,
        mesh=mesh,
        in_specs=(P("energy", "space", None, None, None), P("energy", "space", None, None, None)),
        out_specs=P("energy", "space", None, None, None),
        check_vma=False,
    )
```

profile of v0, /device:TPU:14, one launch (start us, length us, event | category | flops | bytes accessed | tf_op | source)
XLA Modules:
  0.0 103.8 jit_solution(4241025837344211352)
XLA Ops:
  0.0 1.8 %copy.75 = bf16[1,1,3,128,256]{4,2,3,1,0:T(4,128)(2,1)} copy(bf16[1,1,3,128,256]{4,3,2,1,0:T(8,128)(2,1)} %param.2) | data formatting | bytes 393216 | tf_op args[0]
  1.8 0.0 copy-start
  1.8 16.8 %all-to-all-start = ((bf16[1,3,128,256]{3,1,0,2:T(4,128)(2,1)}), bf16[1,3,128,256]{3,1,0,2:T(4,128)(2,1)S(1)}, u32[]{:S(2)}, u32[]{:S(2)}) async-start(bf16[1,3,128,256]{3,1,0,2:T(4,128)(2,1)} %bitcast.62), calls=%async_computation | async-start | bytes 524288 | tf_op jit(solution)/shard_map/all_to_all | solution.py:74
  18.7 0.0 copy-done
  18.7 0.2 copy.25
  18.9 1.9 %collective-permute-start = (bf16[1,1,128,256]{2,3,1,0:T(8,128)(2,1)S(1)}, bf16[1,1,128,256]{2,3,1,0:T(8,128)(2,1)S(1)}, u32[]{:S(2)}, u32[]{:S(2)}) collective-permute-start(bf16[1,1,128,256]{2,3,1,0:T(8,128)(2,1)S(1)} %get-tuple-element.9), channel_id=1, source_target_pairs={{0,32},{32,64},{64,96},{96,128},{128,160},{160,192},{192,224},{224... | collective-permute-start | bytes 196616 | tf_op jit(solution)/shard_map/ppermute | solution.py:14
  20.8 5.1 %collective-permute-start.1 = (bf16[1,1,128,256]{2,3,1,0:T(8,128)(2,1)S(1)}, bf16[1,1,128,256]{2,3,1,0:T(8,128)(2,1)S(1)}, u32[]{:S(2)}, u32[]{:S(2)}) collective-permute-start(bf16[1,1,128,256]{2,3,1,0:T(8,128)(2,1)S(1)} %get-tuple-element.10), channel_id=1, source_target_pairs={{32,0},{64,32},{96,64},{128,96},{160,128},{192,160},{224,192},{256... | collective-permute-start | bytes 196616 | tf_op jit(solution)/shard_map/ppermute | solution.py:17
  25.9 0.2 collective-permute-done
  26.1 1.7 %collective-permute-done.1 = bf16[1,1,128,256]{2,3,1,0:T(8,128)(2,1)S(1)} collective-permute-done((bf16[1,1,128,256]{2,3,1,0:T(8,128)(2,1)S(1)}, bf16[1,1,128,256]{2,3,1,0:T(8,128)(2,1)S(1)}, u32[]{:S(2)}, u32[]{:S(2)}) %collective-permute-start.1) | collective-permute-done | bytes 65568 | tf_op jit(solution)/shard_map/ppermute | solution.py:17
  27.8 0.2 copy.26
  28.0 0.9 copy.27
  28.9 11.3 %all-to-all-done = bf16[1,3,128,256]{3,1,0,2:T(4,128)(2,1)S(1)} async-done(((bf16[1,3,128,256]{3,1,0,2:T(4,128)(2,1)}), bf16[1,3,128,256]{3,1,0,2:T(4,128)(2,1)S(1)}, u32[]{:S(2)}, u32[]{:S(2)}) %all-to-all-start) | async-done | bytes 196640 | tf_op jit(solution)/shard_map/all_to_all | solution.py:74
  40.2 4.1 %all-to-all-start.1 = ((bf16[1,3,128,256]{3,1,0,2:T(4,128)(2,1)}), bf16[1,3,128,256]{3,1,0,2:T(4,128)(2,1)S(1)}, u32[]{:S(2)}, u32[]{:S(2)}) async-start(bf16[1,3,128,256]{3,1,0,2:T(4,128)(2,1)} %copy.27), calls=%async_computation.1 | async-start | bytes 524288 | tf_op jit(solution)/shard_map/all_to_all | solution.py:75
  44.3 0.1 copy.77
  44.4 0.1 reshape.21
  44.4 0.4 fusion.94
  44.8 0.1 copy.23
  45.0 0.1 copy.24
  45.1 0.3 fusion.8
  45.4 0.3 fusion.12
  45.7 0.3 convolution_add_fusion.1
  46.0 21.2 %all-to-all-done.1 = bf16[1,3,128,256]{3,1,0,2:T(4,128)(2,1)S(1)} async-done(((bf16[1,3,128,256]{3,1,0,2:T(4,128)(2,1)}), bf16[1,3,128,256]{3,1,0,2:T(4,128)(2,1)S(1)}, u32[]{:S(2)}, u32[]{:S(2)}) %all-to-all-start.1) | async-done | bytes 196640 | tf_op jit(solution)/shard_map/all_to_all | solution.py:75
  67.2 0.1 copy.76
  67.4 0.1 reshape.24
  67.4 0.3 fusion.92
  67.7 0.1 copy.31
  67.8 0.1 copy.30
  68.0 0.3 fusion.6
  68.3 0.3 fusion.2
  68.6 0.3 convolution_subtract_fusion.1
  68.9 0.3 convolution_add_fusion
  69.2 0.3 multiply_subtract_fusion
  69.5 0.4 fusion.32
  70.0 0.4 fusion.30
  70.4 0.4 fusion.1
  70.9 0.4 fusion
  71.3 0.1 reshape.26
  71.4 0.1 reshape.25
  71.5 0.1 pad_maximum_fusion
  71.6 31.2 %all_to_all.45 = f32[32,3,4,256]{3,2,1,0:T(4,128)S(1)} all-to-all(f32[32,3,4,256]{3,2,1,0:T(4,128)S(1)} %pad_maximum_fusion), channel_id=1, replica_groups=mesh['space'=16,'energy'=32] {'energy'}, dimensions={0} | all-to-all | bytes 786432 | tf_op jit(solution)/shard_map/all_to_all | solution.py:63
  102.9 0.9 broadcast_in_dim.3
  (4 shorter events, 0.1 us)
Async XLA Ops:
  1.8 16.8 %copy-start = (bf16[1,1,3,128,256]{4,3,2,1,0:T(8,128)(2,1)S(1)}, bf16[1,1,3,128,256]{4,3,2,1,0:T(8,128)(2,1)}, u32[]{:S(2)}) copy-start(bf16[1,1,3,128,256]{4,3,2,1,0:T(8,128)(2,1)} %param.3) | copy-start | bytes 589828
  1.8 38.4 %all-to-all-start = ((bf16[1,3,128,256]{3,1,0,2:T(4,128)(2,1)}), bf16[1,3,128,256]{3,1,0,2:T(4,128)(2,1)S(1)}, u32[]{:S(2)}, u32[]{:S(2)}) async-start(bf16[1,3,128,256]{3,1,0,2:T(4,128)(2,1)} %bitcast.62), calls=%async_computation | async-start | bytes 524288 | tf_op jit(solution)/shard_map/all_to_all | solution.py:74
  18.9 7.3 %collective-permute-start = (bf16[1,1,128,256]{2,3,1,0:T(8,128)(2,1)S(1)}, bf16[1,1,128,256]{2,3,1,0:T(8,128)(2,1)S(1)}, u32[]{:S(2)}, u32[]{:S(2)}) collective-permute-start(bf16[1,1,128,256]{2,3,1,0:T(8,128)(2,1)S(1)} %get-tuple-element.9), channel_id=1, source_target_pairs={{0,32},{32,64},{64,96},{96,128},{128,160},{160,192},{192,224},{224... | collective-permute-start | bytes 196616 | tf_op jit(solution)/shard_map/ppermute | solution.py:14
  20.8 7.0 %collective-permute-start.1 = (bf16[1,1,128,256]{2,3,1,0:T(8,128)(2,1)S(1)}, bf16[1,1,128,256]{2,3,1,0:T(8,128)(2,1)S(1)}, u32[]{:S(2)}, u32[]{:S(2)}) collective-permute-start(bf16[1,1,128,256]{2,3,1,0:T(8,128)(2,1)S(1)} %get-tuple-element.10), channel_id=1, source_target_pairs={{32,0},{64,32},{96,64},{128,96},{160,128},{192,160},{224,192},{256... | collective-permute-start | bytes 196616 | tf_op jit(solution)/shard_map/ppermute | solution.py:17
  40.2 27.0 %all-to-all-start.1 = ((bf16[1,3,128,256]{3,1,0,2:T(4,128)(2,1)}), bf16[1,3,128,256]{3,1,0,2:T(4,128)(2,1)S(1)}, u32[]{:S(2)}, u32[]{:S(2)}) async-start(bf16[1,3,128,256]{3,1,0,2:T(4,128)(2,1)} %copy.27), calls=%async_computation.1 | async-start | bytes 524288 | tf_op jit(solution)/shard_map/all_to_all | solution.py:75
where the time goes:
time: 104 us
  waiting for transfers between devices  34.4 us (33%)
  blocking collectives  31.2 us (30%)
  starting transfers between devices  28 us (27%)
  local copies, waits for them, and re-layouts  5.54 us (5%)
  matrix products  4.23 us (4%)
    all_to_all x1, blocking collectives, correlate_rows(): lax.all_to_all(result, 'energy', split_axis=0, concat_axis=2, tiled=True)  31.2 us
    all_to_all x1, waiting for transfers between devices, on_device(): lax.all_to_all(mirrored, 'energy', split_axis=2, concat_axis=0, tiled=True)  21.2 us
    all_to_all x1, starting transfers between devices, on_device(): lax.all_to_all(own_lesser, 'energy', split_axis=2, concat_axis=0, tiled=T...  16.8 us
    all_to_all x1, waiting for transfers between devices, on_device(): lax.all_to_all(own_lesser, 'energy', split_axis=2, concat_axis=0, tiled=T...  11.3 us
    ppermute x1, starting transfers between devices, with_halo(): lax.ppermute(lax.slice_in_dim(block, 0, width, axis=dim), axis, backward)  5.15 us
    dot_general x12, matrix products, apply(): jnp.dot(matrix, data, precision=high, preferred_element_type=jnp.float32)  4.23 us
    all_to_all x1, starting transfers between devices, on_device(): lax.all_to_all(mirrored, 'energy', split_axis=2, concat_axis=0, tiled=True)  4.09 us
  transfers between devices with their start and end apart: 4, of which 4 were waited for; matrix products, arithmetic and copies ran while one was open for 3% of the time, Pallas kernels for 0%

commit v1 on v0

v1 whole, which is shorter than its diff:
```python
import functools
import math

import jax
import jax.numpy as jnp
from jax import lax
from jax.experimental import pallas as pl
from jax.experimental.pallas import tpu as pltpu
from jax.sharding import PartitionSpec as P

MESH = pl.DeviceIdType.MESH
F32 = jnp.float32

BOUND = 405.0 * 1.002
STEEP, SHALLOW, KNEE = 13.2, 5.0, 10.0
TOP = 127.0
SHIFT = (STEEP - SHALLOW) * KNEE


def encode(value, scale):
    part = jnp.abs(value) * scale
    octave = jnp.log2(jnp.maximum(part, 2.0**-33))
    code = jnp.exp2(TOP + jnp.maximum(STEEP * octave, SHALLOW * octave - SHIFT))
    code = jnp.where(part < 2.0**-33, 0.0, code)
    return jnp.where(value < 0, -code, code)


def decode(code, bound):
    size = jnp.abs(code)
    level = jnp.log2(jnp.maximum(size, 2.0**-126)) - TOP
    octave = jnp.minimum(level * (1.0 / STEEP), (level + SHIFT) * (1.0 / SHALLOW))
    value = jnp.exp2(octave) * bound
    value = jnp.where(size == 0, 0.0, value)
    return jnp.where(code < 0, -value, value)


def cadd(a, b):
    return a[0] + b[0], a[1] + b[1]


def csub(a, b):
    return a[0] - b[0], a[1] - b[1]


def turn(a, step, total):
    step = step % total
    eighth = 8 * step
    re, im = a
    if eighth % total == 0:
        way = eighth // total
        if way % 2 == 0:
            return [(re, im), (im, -re), (-re, -im), (-im, re)][way // 2]
        half = math.sqrt(0.5)
        p, m = (re + im) * half, (im - re) * half
        return {1: (p, m), 3: (m, -p), 5: (-p, -m), 7: (-m, p)}[way]
    c = math.cos(2 * math.pi * step / total)
    s = math.sin(2 * math.pi * step / total)
    return re * c + im * s, im * c - re * s


def fft(values, sign):
    n = len(values)
    if n == 1:
        return values
    even, odd = fft(values[0::2], sign), fft(values[1::2], sign)
    odd = [turn(v, sign * k, n) for k, v in enumerate(odd)]
    return [cadd(a, b) for a, b in zip(even, odd)] + [csub(a, b) for a, b in zip(even, odd)]


def kernel(
    n_space, n_energy,
    l_ref, g_ref, o_ref,
    halo, own, mirror, lbuf, gbuf, work, wide, code, back,
    own_sem, halo_send, halo_recv, lsend, gsend, lrecv, grecv, psend, precv,
):
    space, me = lax.axis_index("space"), lax.axis_index("energy")
    core = lax.rem(space, 2)
    plane, side = me // 2, lax.rem(me, 2)
    up, down = lax.rem(space + 1, n_space), lax.rem(space + n_space - 1, n_space)

    def owner(unit):
        late = unit - 16
        z = jnp.where(unit < 16, unit, 4 * (late // 2) + lax.rem(late, 2) + 2 * core)
        x = lax.rem(lax.rem(z, 2) + core + jnp.where(unit < 16, 0, 1), 2)
        return 2 * z + x

    first = side == lax.rem(plane + core, 2)
    rest = lax.rem(plane, 4) - 2 * core
    second = jnp.logical_and(jnp.logical_not(first), jnp.logical_or(rest == 0, rest == 1))
    unit_here = jnp.where(first, plane, 16 + 2 * (plane // 4) + rest)
    works = jnp.logical_or(first, second)

    barrier = pltpu.get_barrier_semaphore()
    pl.semaphore_signal(barrier, inc=1, device_id=(up, me), device_id_type=MESH)
    pl.semaphore_signal(barrier, inc=1, device_id=(down, me), device_id_type=MESH)

    @pl.loop(1, n_energy)
    def _(k):
        pl.semaphore_signal(
            barrier, inc=1, device_id=(space, lax.rem(me + k, n_energy)), device_id_type=MESH
        )

    own_copy = pltpu.make_async_copy(g_ref.at[0, 0, 1], own, own_sem)
    own_copy.start()

    def flipped(tile):
        tile = tile.astype(F32)
        return jnp.concatenate([tile[:, :128].T, tile[:, 128:].T], axis=1)

    own_copy.wait()
    mirror[1] = flipped(own[...]).astype(jnp.bfloat16)
    pl.semaphore_wait(barrier, n_energy + 1)

    halos = [
        pltpu.make_async_remote_copy(
            g_ref.at[0, 0, 2 - 2 * i], halo.at[i], halo_send.at[i], halo_recv.at[i],
            device_id=(dest, me), device_id_type=MESH,
        )
        for i, dest in ((0, up), (1, down))
    ]
    for copy in halos:
        copy.start()

    def unit_rows(unit):
        return unit // 8, pl.ds(pl.multiple_of(lax.rem(unit, 8) * 16, 16), 16)

    def spread(source, target, send, recv, start, count):
        @pl.loop(0, count)
        def _(k):
            unit = start + lax.rem(plane + k, count)
            dest = owner(unit)
            t, rows = unit_rows(unit)

            @pl.when(dest != me)
            def _():
                pltpu.make_async_remote_copy(
                    source.at[t, rows], target.at[me], send.at[unit], recv,
                    device_id=(space, dest), device_id_type=MESH,
                ).start()

            @pl.when(dest == me)
            def _():
                pltpu.make_async_copy(source.at[t, rows], target.at[me], recv).start()

    lesser = l_ref.at[0, 0]
    spread(lesser, lbuf, lsend, lrecv, 0, 16)
    halos[0].wait_recv()
    left = flipped(halo[0])
    mirror[0] = jnp.where(space > 0, left, 0.0).astype(jnp.bfloat16)
    spread(mirror, gbuf, gsend, grecv, 0, 16)
    spread(lesser, lbuf, lsend, lrecv, 16, 8)
    halos[1].wait_recv()
    right = flipped(halo[1])
    mirror[2] = jnp.where(space < n_space - 1, right, 0.0).astype(jnp.bfloat16)
    spread(mirror, gbuf, gsend, grecv, 16, 8)

    scale = 1.0 / (n_energy * BOUND)

    @pl.when(works)
    def _():
        pltpu.make_async_copy(lbuf, lbuf, lrecv).wait()
        pltpu.make_async_copy(gbuf, gbuf, grecv).wait()

        def read(ref, e):
            pair = ref[e].astype(F32)
            return pair[:, :128], pair[:, 128:]

        for part, (ref, sign) in enumerate(((lbuf, 1), (gbuf, -1))):
            for r in range(4):
                out = fft([read(ref, 4 * a + r) for a in range(8)], sign)
                for s, v in enumerate(out):
                    v = turn(v, sign * r * s, 32)
                    work[part, 4 * s + r, :, :128] = v[0]
                    work[part, 4 * s + r, :, 128:] = v[1]
        for s in range(8):
            hats = []
            for part, sign in ((0, 1), (1, -1)):
                pairs = [
                    (work[part, 4 * s + r, :, :128], work[part, 4 * s + r, :, 128:]) for r in range(4)
                ]
                hats.append(fft(pairs, sign))
            prods = [
                (a[0] * b[0] - a[1] * b[1], a[0] * b[1] + a[1] * b[0]) for a, b in zip(*hats)
            ]
            for r, v in enumerate(fft(prods, -1)):
                v = turn(v, -r * s, 32)
                wide[8 * r + s, :, :128] = v[0]
                wide[8 * r + s, :, 128:] = v[1]
        for r in range(4):
            pairs = [(wide[8 * r + s, :, :128], wide[8 * r + s, :, 128:]) for s in range(8)]
            for a, v in enumerate(fft(pairs, -1)):
                code[4 * a + r] = encode(jnp.concatenate(v, axis=1), scale).astype(jnp.bfloat16)

        @pl.loop(1, n_energy)
        def _(k):
            dest = lax.rem(me + k, n_energy)
            pltpu.make_async_remote_copy(
                code.at[dest], back.at[unit_here], psend.at[dest], precv.at[unit_here],
                device_id=(space, dest), device_id_type=MESH,
            ).start()

        pltpu.make_async_copy(code.at[me], back.at[unit_here], precv.at[unit_here]).start()

    @pl.loop(0, 24)
    def _(k):
        unit = jnp.where(k < 16, lax.rem(plane + k, 16), k)
        t, rows = unit_rows(unit)
        pltpu.make_async_copy(back.at[unit], back.at[unit], precv.at[unit]).wait()
        o_ref[0, 0, t, rows, :] = decode(back[unit].astype(F32), BOUND)

    for copy in halos:
        copy.wait_send()

    @pl.loop(0, 24)
    def _(unit):
        dest = owner(unit)

        @pl.when(dest != me)
        def _():
            for source, send in ((lbuf, lsend), (gbuf, gsend)):
                pltpu.make_async_copy(source.at[0], source.at[0], send.at[unit]).wait()

    @pl.when(works)
    def _():
        @pl.loop(1, n_energy)
        def _(k):
            dest = lax.rem(me + k, n_energy)
            pltpu.make_async_copy(code.at[dest], code.at[dest], psend.at[dest]).wait()


def on_device(n_space, n_energy, lesser, greater):
    unit = (16, 256)
    dma = pltpu.SemaphoreType.DMA
    return pl.pallas_call(
        functools.partial(kernel, n_space, n_energy),
        out_shape=jax.ShapeDtypeStruct(lesser.shape, F32),
        in_specs=[pl.BlockSpec(memory_space=pltpu.HBM)] * 2,
        out_specs=pl.BlockSpec(memory_space=pltpu.VMEM),
        scratch_shapes=[
            pltpu.VMEM((2, 128, 256), jnp.bfloat16),
            pltpu.VMEM((128, 256), jnp.bfloat16),
            pltpu.VMEM((3, 128, 256), jnp.bfloat16),
            pltpu.VMEM((n_energy, *unit), jnp.bfloat16),
            pltpu.VMEM((n_energy, *unit), jnp.bfloat16),
            pltpu.VMEM((2, n_energy, *unit), F32),
            pltpu.VMEM((n_energy, *unit), F32),
            pltpu.VMEM((n_energy, *unit), jnp.bfloat16),
            pltpu.VMEM((24, *unit), jnp.bfloat16),
            dma,
            dma((2,)),
            dma((2,)),
            dma((24,)),
            dma((24,)),
            dma,
            dma,
            dma((n_energy,)),
            dma((24,)),
        ],
        compiler_params=pltpu.CompilerParams(
            collective_id=0, has_side_effects=True, vmem_limit_bytes=32 << 20
        ),
    )(lesser, greater)


def solution(mesh):
    spec = P("energy", "space", None, None, None)
    return jax.shard_map(
        functools.partial(on_device, mesh.shape["space"], mesh.shape["energy"]),
        mesh=mesh,
        in_specs=(spec, spec),
        out_specs=spec,
        check_vma=False,
    )
```

time: 104 us -> 55.4 us (0.53)
  the two profiles are of different devices: /device:TPU:14 before, /device:TPU:16 now
where the time goes in v1:
time: 55.4 us; the launch traced here: 55.2 us
  Pallas kernels  52.6 us (95%)
  local copies, waits for them, and re-layouts  2.6 us (5%)
    pallas_call x1, Pallas kernels, on_device(): pl.pallas_call(functools.partial(kernel, n_space, n_energy), out_shape=ja...  52.6 us
    unnamed x5, local copies, waits for them, and re-layouts  2.6 us

profile of v1, /device:TPU:16, one launch (start us, length us, event | category | flops | bytes accessed | tf_op | source)
XLA Modules:
  0.0 55.2 jit_solution(3630374633735045509)
XLA Ops:
  0.0 0.0 copy-start
  0.0 0.9 %copy-done = bf16[1,1,3,128,256]{4,3,2,1,0:T(8,128)(2,1)S(1)} copy-done((bf16[1,1,3,128,256]{4,3,2,1,0:T(8,128)(2,1)S(1)}, bf16[1,1,3,128,256]{4,3,2,1,0:T(8,128)(2,1)}, u32[]{:S(2)}) %copy-start) | copy-done | bytes 196632
  0.9 0.0 copy-start.1
  0.9 0.9 %copy-done.1 = bf16[1,1,3,128,256]{4,3,2,1,0:T(8,128)(2,1)S(1)} copy-done((bf16[1,1,3,128,256]{4,3,2,1,0:T(8,128)(2,1)S(1)}, bf16[1,1,3,128,256]{4,3,2,1,0:T(8,128)(2,1)}, u32[]{:S(2)}) %copy-start.1) | copy-done | bytes 196632
  1.9 52.6 %shard_map.28 = f32[1,1,3,128,256]{4,3,2,1,0:T(8,128)S(1)} custom-call(bf16[1,1,3,128,256]{4,3,2,1,0:T(8,128)(2,1)S(1)} %copy-done, bf16[1,1,3,128,256]{4,3,2,1,0:T(8,128)(2,1)S(1)} %copy-done.1), custom_call_target="tpu_custom_call" | custom-call | tf_op jit(solution)/shard_map/pallas_call | solution.py:234
  54.5 0.7 %copy.4 = f32[1,1,3,128,256]{4,3,2,1,0:T(8,128)} copy(f32[1,1,3,128,256]{4,3,2,1,0:T(8,128)S(1)} %shard_map.28) | data formatting | bytes 786432
Async XLA Ops:
  0.0 0.9 %copy-start = (bf16[1,1,3,128,256]{4,3,2,1,0:T(8,128)(2,1)S(1)}, bf16[1,1,3,128,256]{4,3,2,1,0:T(8,128)(2,1)}, u32[]{:S(2)}) copy-start(bf16[1,1,3,128,256]{4,3,2,1,0:T(8,128)(2,1)} %l_ref.1) | copy-start | bytes 589828
  0.9 0.9 %copy-start.1 = (bf16[1,1,3,128,256]{4,3,2,1,0:T(8,128)(2,1)S(1)}, bf16[1,1,3,128,256]{4,3,2,1,0:T(8,128)(2,1)}, u32[]{:S(2)}) copy-start(bf16[1,1,3,128,256]{4,3,2,1,0:T(8,128)(2,1)} %g_ref.1) | copy-start | bytes 589828

commit v2 on v1

--- a/solution.py
+++ b/solution.py
@@ -70,7 +70,7 @@
 def kernel(
     n_space, n_energy,
     l_ref, g_ref, o_ref,
-    halo, own, mirror, lbuf, gbuf, work, wide, code, back,
+    halo, local, mirror, lbuf, gbuf, work, wide, code,
     own_sem, halo_send, halo_recv, lsend, gsend, lrecv, grecv, psend, precv,
 ):
     space, me = lax.axis_index("space"), lax.axis_index("energy")
@@ -78,18 +78,16 @@
     plane, side = me // 2, lax.rem(me, 2)
     up, down = lax.rem(space + 1, n_space), lax.rem(space + n_space - 1, n_space)
 
-    def owner(unit):
-        late = unit - 16
-        z = jnp.where(unit < 16, unit, 4 * (late // 2) + lax.rem(late, 2) + 2 * core)
-        x = lax.rem(lax.rem(z, 2) + core + jnp.where(unit < 16, 0, 1), 2)
-        return 2 * z + x
-
     first = side == lax.rem(plane + core, 2)
     rest = lax.rem(plane, 4) - 2 * core
     second = jnp.logical_and(jnp.logical_not(first), jnp.logical_or(rest == 0, rest == 1))
     unit_here = jnp.where(first, plane, 16 + 2 * (plane // 4) + rest)
     works = jnp.logical_or(first, second)
 
+    l_copy = pltpu.make_async_copy(l_ref.at[0, 0], local.at[pl.ds(0, 3)], own_sem.at[0])
+    own_copy = pltpu.make_async_copy(g_ref.at[0, 0, 1], local.at[3], own_sem.at[1])
+    l_copy.start()
+    own_copy.start()
     barrier = pltpu.get_barrier_semaphore()
     pl.semaphore_signal(barrier, inc=1, device_id=(up, me), device_id_type=MESH)
     pl.semaphore_signal(barrier, inc=1, device_id=(down, me), device_id_type=MESH)
@@ -100,15 +98,10 @@
             barrier, inc=1, device_id=(space, lax.rem(me + k, n_energy)), device_id_type=MESH
         )
 
-    own_copy = pltpu.make_async_copy(g_ref.at[0, 0, 1], own, own_sem)
-    own_copy.start()
-
     def flipped(tile):
         tile = tile.astype(F32)
         return jnp.concatenate([tile[:, :128].T, tile[:, 128:].T], axis=1)
 
-    own_copy.wait()
-    mirror[1] = flipped(own[...]).astype(jnp.bfloat16)
     pl.semaphore_wait(barrier, n_energy + 1)
 
     halos = [
@@ -124,35 +117,74 @@
     def unit_rows(unit):
         return unit // 8, pl.ds(pl.multiple_of(lax.rem(unit, 8) * 16, 16), 16)
 
-    def spread(source, target, send, recv, start, count):
-        @pl.loop(0, count)
-        def _(k):
-            unit = start + lax.rem(plane + k, count)
-            dest = owner(unit)
-            t, rows = unit_rows(unit)
-
-            @pl.when(dest != me)
-            def _():
-                pltpu.make_async_remote_copy(
-                    source.at[t, rows], target.at[me], send.at[unit], recv,
-                    device_id=(space, dest), device_id_type=MESH,
-                ).start()
-
-            @pl.when(dest == me)
-            def _():
-                pltpu.make_async_copy(source.at[t, rows], target.at[me], recv).start()
-
-    lesser = l_ref.at[0, 0]
-    spread(lesser, lbuf, lsend, lrecv, 0, 16)
+    def plane_at(k):
+        away = 8 + jnp.where(lax.rem(k, 2) == 0, k // 2, -((k + 1) // 2))
+        return lax.rem(plane + away, 16)
+
+    def has_second(z):
+        late = lax.rem(z, 4) - 2 * core
+        return jnp.logical_or(late == 0, late == 1)
+
+    def unit_of(z, which):
+        return z if which == 0 else 16 + 2 * (z // 4) + lax.rem(lax.rem(z, 4), 2)
+
+    def owner_of(z, which):
+        return 2 * z + lax.rem(lax.rem(z, 2) + core + which, 2)
+
+    def send(source, target, sems, recv, z, which):
+        unit, dest = unit_of(z, which), owner_of(z, which)
+        t, rows = unit_rows(unit)
+
+        @pl.when(dest != me)
+        def _():
+            pltpu.make_async_remote_copy(
+                source.at[t, rows], target.at[me], sems.at[unit], recv,
+                device_id=(space, dest), device_id_type=MESH,
+            ).start()
+
+        @pl.when(dest == me)
+        def _():
+            pltpu.make_async_copy(source.at[t, rows], target.at[me], recv).start()
+
+    def sent(source, sems, z, which):
+        @pl.when(owner_of(z, which) != me)
+        def _():
+            pltpu.make_async_copy(source.at[0], source.at[0], sems.at[unit_of(z, which)]).wait()
+
+    l_copy.wait()
+
+    @pl.loop(0, 16)
+    def _(k):
+        z = plane_at(k)
+        send(local, lbuf, lsend, lrecv, z, 0)
+
+        @pl.when(has_second(z))
+        def _():
+            send(local, lbuf, lsend, lrecv, z, 1)
+
+    own_copy.wait()
+    mirror[1] = flipped(local[3]).astype(jnp.bfloat16)
     halos[0].wait_recv()
     left = flipped(halo[0])
     mirror[0] = jnp.where(space > 0, left, 0.0).astype(jnp.bfloat16)
-    spread(mirror, gbuf, gsend, grecv, 0, 16)
-    spread(lesser, lbuf, lsend, lrecv, 16, 8)
     halos[1].wait_recv()
     right = flipped(halo[1])
     mirror[2] = jnp.where(space < n_space - 1, right, 0.0).astype(jnp.bfloat16)
-    spread(mirror, gbuf, gsend, grecv, 16, 8)
+
+    @pl.loop(0, 16)
+    def _(k):
+        z = plane_at(k)
+        sent(lbuf, lsend, z, 0)
+        send(mirror, gbuf, gsend, grecv, z, 0)
+
+        @pl.when(has_second(z))
+        def _():
+            sent(lbuf, lsend, z, 1)
+            send(mirror, gbuf, gsend, grecv, z, 1)
+
+    @pl.loop(0, 16)
+    def _(k):
+        sent(gbuf, gsend, plane_at(k), 0)
 
     scale = 1.0 / (n_energy * BOUND)
 
@@ -191,34 +223,34 @@
             for a, v in enumerate(fft(pairs, -1)):
                 code[4 * a + r] = encode(jnp.concatenate(v, axis=1), scale).astype(jnp.bfloat16)
 
-        @pl.loop(1, n_energy)
+        def give(dest):
+            @pl.when(dest != me)
+            def _():
+                pltpu.make_async_remote_copy(
+                    code.at[dest], o_ref.at[unit_here], psend.at[dest], precv.at[unit_here],
+                    device_id=(space, dest), device_id_type=MESH,
+                ).start()
+
+            @pl.when(dest == me)
+            def _():
+                pltpu.make_async_copy(code.at[dest], o_ref.at[unit_here], precv.at[unit_here]).start()
+
+        @pl.loop(0, 32)
         def _(k):
-            dest = lax.rem(me + k, n_energy)
-            pltpu.make_async_remote_copy(
-                code.at[dest], back.at[unit_here], psend.at[dest], precv.at[unit_here],
-                device_id=(space, dest), device_id_type=MESH,
-            ).start()
-
-        pltpu.make_async_copy(code.at[me], back.at[unit_here], precv.at[unit_here]).start()
+            give(k)
 
     @pl.loop(0, 24)
     def _(k):
-        unit = jnp.where(k < 16, lax.rem(plane + k, 16), k)
-        t, rows = unit_rows(unit)
-        pltpu.make_async_copy(back.at[unit], back.at[unit], precv.at[unit]).wait()
-        o_ref[0, 0, t, rows, :] = decode(back[unit].astype(F32), BOUND)
+        pltpu.make_async_copy(o_ref.at[k], o_ref.at[k], precv.at[k]).wait()
 
     for copy in halos:
         copy.wait_send()
 
-    @pl.loop(0, 24)
-    def _(unit):
-        dest = owner(unit)
-
-        @pl.when(dest != me)
-        def _():
-            for source, send in ((lbuf, lsend), (gbuf, gsend)):
-                pltpu.make_async_copy(source.at[0], source.at[0], send.at[unit]).wait()
+    @pl.loop(0, 16)
+    def _(z):
+        @pl.when(has_second(z))
+        def _():
+            sent(gbuf, gsend, z, 1)
 
     @pl.when(works)
     def _():
@@ -231,22 +263,21 @@
 def on_device(n_space, n_energy, lesser, greater):
     unit = (16, 256)
     dma = pltpu.SemaphoreType.DMA
-    return pl.pallas_call(
+    codes = pl.pallas_call(
         functools.partial(kernel, n_space, n_energy),
-        out_shape=jax.ShapeDtypeStruct(lesser.shape, F32),
+        out_shape=pltpu.VMEM((24, *unit), jnp.bfloat16),
         in_specs=[pl.BlockSpec(memory_space=pltpu.HBM)] * 2,
         out_specs=pl.BlockSpec(memory_space=pltpu.VMEM),
         scratch_shapes=[
             pltpu.VMEM((2, 128, 256), jnp.bfloat16),
-            pltpu.VMEM((128, 256), jnp.bfloat16),
+            pltpu.VMEM((4, 128, 256), jnp.bfloat16),
             pltpu.VMEM((3, 128, 256), jnp.bfloat16),
             pltpu.VMEM((n_energy, *unit), jnp.bfloat16),
             pltpu.VMEM((n_energy, *unit), jnp.bfloat16),
             pltpu.VMEM((2, n_energy, *unit), F32),
             pltpu.VMEM((n_energy, *unit), F32),
             pltpu.VMEM((n_energy, *unit), jnp.bfloat16),
-            pltpu.VMEM((24, *unit), jnp.bfloat16),
-            dma,
+            dma((2,)),
             dma((2,)),
             dma((2,)),
             dma((24,)),
@@ -257,9 +288,10 @@
             dma((24,)),
         ],
         compiler_params=pltpu.CompilerParams(
-            collective_id=0, has_side_effects=True, vmem_limit_bytes=32 << 20
+            collective_id=0, has_side_effects=True, vmem_limit_bytes=62 << 20
         ),
     )(lesser, greater)
+    return decode(codes.reshape(lesser.shape).astype(F32), BOUND)
 
 
 def solution(mesh):

time: 55.4 us -> 47.5 us (0.86)
  Pallas kernels: 52.6 us -> 46.2 us
  local copies, waits for them, and re-layouts: 2.6 us -> 0 us
  other arithmetic: 0 us -> 1.1 us
    pallas_call x1, Pallas kernels: 52.6 us -> 46.2 us  [on_device(): pl.pallas_call(functools.partial(kernel, n_space, n_energy), out_shape=pl...]
    unnamed x5 -> x0, local copies, waits for them, and re-layouts: 2.6 us -> none
    select_n x0 -> x2, other arithmetic: none -> 1.03 us  [the longest x1 0.8 us: decode(): return jnp.where(code < 0, -value, value)]
where the time goes in v2:
time: 47.5 us; the launch traced here: 47.3 us
  Pallas kernels  46.2 us (97%)
  other arithmetic  1.1 us (2%)
    pallas_call x1, Pallas kernels, on_device(): pl.pallas_call(functools.partial(kernel, n_space, n_energy), out_shape=pl...  46.2 us

profile of v2, /device:TPU:16, one launch (start us, length us, event | category | flops | bytes accessed | tf_op | source)
XLA Modules:
  0.0 47.3 jit_solution(12525156465355552579)
XLA Ops:
  0.0 46.2 %shard_map.28 = bf16[24,16,256]{2,1,0:T(8,128)(2,1)S(1)} custom-call(bf16[1,1,3,128,256]{4,3,2,1,0:T(8,128)(2,1)} %l_ref.1, bf16[1,1,3,128,256]{4,3,2,1,0:T(8,128)(2,1)} %g_ref.1), custom_call_target="tpu_custom_call" | custom-call | tf_op jit(solution)/shard_map/pallas_call | solution.py:266
  46.2 0.1 convert_compare_fusion
  46.3 0.2 fusion.11
  46.5 0.8 %negate_select_fusion = f32[1,1,3,128,256]{4,3,2,1,0:T(8,128)} fusion(pred[1,1,3,128,256]{4,3,2,1,0:T(8,128)(4,1)S(1)} %bitcast.3, f32[1,1,3,128,256]{4,3,2,1,0:T(8,128)S(1)} %bitcast.2), kind=kLoop, calls=%fused_computation | loop fusion | flops 196608 | bytes 884736 | tf_op jit(solution)/shard_map/jit(_where)/select_n | solution.py:34

commit v3 on v2

--- a/solution.py
+++ b/solution.py
@@ -9,6 +9,7 @@
 from jax.sharding import PartitionSpec as P
 
 MESH = pl.DeviceIdType.MESH
+REACH, STEPS = 4, 1
 F32 = jnp.float32
 
 BOUND = 405.0 * 1.002
@@ -71,7 +72,7 @@
     n_space, n_energy,
     l_ref, g_ref, o_ref,
     halo, local, mirror, lbuf, gbuf, work, wide, code,
-    own_sem, halo_send, halo_recv, lsend, gsend, lrecv, grecv, psend, precv,
+    own_sem, halo_send, halo_recv, lsend, gsend, lrecv, grecv, psend, precv, from_behind, from_ahead,
 ):
     space, me = lax.axis_index("space"), lax.axis_index("energy")
     core = lax.rem(space, 2)
@@ -92,17 +93,29 @@
     pl.semaphore_signal(barrier, inc=1, device_id=(up, me), device_id_type=MESH)
     pl.semaphore_signal(barrier, inc=1, device_id=(down, me), device_id_type=MESH)
 
-    @pl.loop(1, n_energy)
+
+    @pl.loop(0, 2 * (2 * REACH + 1))
     def _(k):
-        pl.semaphore_signal(
-            barrier, inc=1, device_id=(space, lax.rem(me + k, n_energy)), device_id_type=MESH
-        )
+        peer = lax.rem(2 * plane + n_energy - 2 * REACH + k, n_energy)
+
+        @pl.when(peer != me)
+        def _():
+            pl.semaphore_signal(barrier, inc=1, device_id=(space, peer), device_id_type=MESH)
+
+    ahead = (space, lax.rem(me + 2 * REACH, n_energy))
+    behind = (space, lax.rem(me + n_energy - 2 * REACH, n_energy))
 
     def flipped(tile):
         tile = tile.astype(F32)
         return jnp.concatenate([tile[:, :128].T, tile[:, 128:].T], axis=1)
 
-    pl.semaphore_wait(barrier, n_energy + 1)
+    pl.semaphore_wait(barrier, 2 * (2 * REACH + 1) + 1)
+
+    def tell(sem, peer):
+        pl.semaphore_signal(sem, inc=1, device_id=peer, device_id_type=MESH)
+
+    tell(from_behind.at[1], ahead)
+    tell(from_ahead.at[1], behind)
 
     halos = [
         pltpu.make_async_remote_copy(
@@ -153,15 +166,35 @@
 
     l_copy.wait()
 
-    @pl.loop(0, 16)
-    def _(k):
-        z = plane_at(k)
+    def send_lesser(z):
         send(local, lbuf, lsend, lrecv, z, 0)
 
         @pl.when(has_second(z))
         def _():
             send(local, lbuf, lsend, lrecv, z, 1)
 
+    def send_greater(z):
+        send(mirror, gbuf, gsend, grecv, z, 0)
+
+        @pl.when(has_second(z))
+        def _():
+            send(mirror, gbuf, gsend, grecv, z, 1)
+
+    def around(act, distances):
+        for k in distances:
+            act(lax.rem(plane + 16 - k, 16))
+            if k % 8:
+                act(lax.rem(plane + k, 16))
+
+    def hear(step):
+        for sem, peer in ((from_behind, ahead), (from_ahead, behind)):
+            pl.semaphore_wait(sem.at[step], 1)
+            if step < STEPS:
+                tell(sem.at[step + 1], peer)
+
+    around(send_lesser, (4, 3, 2, 1, 0))
+    hear(1)
+    around(send_lesser, (8, 7, 6, 5))
     own_copy.wait()
     mirror[1] = flipped(local[3]).astype(jnp.bfloat16)
     halos[0].wait_recv()
@@ -170,21 +203,7 @@
     halos[1].wait_recv()
     right = flipped(halo[1])
     mirror[2] = jnp.where(space < n_space - 1, right, 0.0).astype(jnp.bfloat16)
-
-    @pl.loop(0, 16)
-    def _(k):
-        z = plane_at(k)
-        sent(lbuf, lsend, z, 0)
-        send(mirror, gbuf, gsend, grecv, z, 0)
-
-        @pl.when(has_second(z))
-        def _():
-            sent(lbuf, lsend, z, 1)
-            send(mirror, gbuf, gsend, grecv, z, 1)
-
-    @pl.loop(0, 16)
-    def _(k):
-        sent(gbuf, gsend, plane_at(k), 0)
+    around(send_greater, (8, 7, 6, 5, 4, 3, 2, 1, 0))
 
     scale = 1.0 / (n_energy * BOUND)
 
@@ -248,8 +267,12 @@
 
     @pl.loop(0, 16)
     def _(z):
+        sent(lbuf, lsend, z, 0)
+        sent(gbuf, gsend, z, 0)
+
         @pl.when(has_second(z))
         def _():
+            sent(lbuf, lsend, z, 1)
             sent(gbuf, gsend, z, 1)
 
     @pl.when(works)
@@ -286,6 +309,8 @@
             dma,
             dma((n_energy,)),
             dma((24,)),
+            pltpu.SemaphoreType.REGULAR((9,)),
+            pltpu.SemaphoreType.REGULAR((9,)),
         ],
         compiler_params=pltpu.CompilerParams(
             collective_id=0, has_side_effects=True, vmem_limit_bytes=62 << 20

time: 47.5 us -> 46.4 us (0.977)
  the two profiles are of different devices: /device:TPU:16 before, /device:TPU:56 now
where the time goes in v3:
time: 46.4 us; the launch traced here: 46.3 us
  Pallas kernels  45.1 us (97%)
  other arithmetic  1.1 us (2%)
    pallas_call x1, Pallas kernels, on_device(): pl.pallas_call(functools.partial(kernel, n_space, n_energy), out_shape=pl...  45.1 us

profile of v3, /device:TPU:56, one launch (start us, length us, event | category | flops | bytes accessed | tf_op | source)
XLA Modules:
  0.0 46.3 jit_solution(2816714083421951758)
XLA Ops:
  0.0 45.1 %shard_map.28 = bf16[24,16,256]{2,1,0:T(8,128)(2,1)S(1)} custom-call(bf16[1,1,3,128,256]{4,3,2,1,0:T(8,128)(2,1)} %l_ref.1, bf16[1,1,3,128,256]{4,3,2,1,0:T(8,128)(2,1)} %g_ref.1), custom_call_target="tpu_custom_call" | custom-call | tf_op jit(solution)/shard_map/pallas_call | solution.py:289
  45.2 0.1 convert_compare_fusion
  45.2 0.2 fusion.11
  45.5 0.8 %negate_select_fusion = f32[1,1,3,128,256]{4,3,2,1,0:T(8,128)} fusion(pred[1,1,3,128,256]{4,3,2,1,0:T(8,128)(4,1)S(1)} %bitcast.3, f32[1,1,3,128,256]{4,3,2,1,0:T(8,128)S(1)} %bitcast.2), kind=kLoop, calls=%fused_computation | loop fusion | flops 196608 | bytes 884736 | tf_op jit(solution)/shard_map/jit(_where)/select_n | solution.py:35

commit v4 on v3

--- a/solution.py
+++ b/solution.py
@@ -12,7 +12,7 @@
 REACH, STEPS = 4, 1
 F32 = jnp.float32
 
-BOUND = 405.0 * 1.002
+MARGIN = 64.2
 STEEP, SHALLOW, KNEE = 13.2, 5.0, 10.0
 TOP = 127.0
 SHIFT = (STEEP - SHALLOW) * KNEE
@@ -71,8 +71,8 @@
 def kernel(
     n_space, n_energy,
     l_ref, g_ref, o_ref,
-    halo, local, mirror, lbuf, gbuf, work, wide, code,
-    own_sem, halo_send, halo_recv, lsend, gsend, lrecv, grecv, psend, precv, from_behind, from_ahead,
+    halo, local, mirror, lbuf, gbuf, work, wide, code, back, bound_out, bound_in,
+    own_sem, halo_send, halo_recv, lsend, gsend, lrecv, grecv, psend, precv, bsend, brecv, from_behind, from_ahead,
 ):
     space, me = lax.axis_index("space"), lax.axis_index("energy")
     core = lax.rem(space, 2)
@@ -205,8 +205,6 @@
     mirror[2] = jnp.where(space < n_space - 1, right, 0.0).astype(jnp.bfloat16)
     around(send_greater, (8, 7, 6, 5, 4, 3, 2, 1, 0))
 
-    scale = 1.0 / (n_energy * BOUND)
-
     @pl.when(works)
     def _():
         pltpu.make_async_copy(lbuf, lbuf, lrecv).wait()
@@ -216,13 +214,23 @@
             pair = ref[e].astype(F32)
             return pair[:, :128], pair[:, 128:]
 
+        tops = []
         for part, (ref, sign) in enumerate(((lbuf, 1), (gbuf, -1))):
+            top = jnp.zeros((16, 128), F32)
             for r in range(4):
-                out = fft([read(ref, 4 * a + r) for a in range(8)], sign)
+                pairs = [read(ref, 4 * a + r) for a in range(8)]
+                for v in pairs:
+                    top = jnp.maximum(top, jnp.maximum(jnp.abs(v[0]), jnp.abs(v[1])))
+                out = fft(pairs, sign)
                 for s, v in enumerate(out):
                     v = turn(v, sign * r * s, 32)
                     work[part, 4 * s + r, :, :128] = v[0]
                     work[part, 4 * s + r, :, 128:] = v[1]
+            tops.append(jnp.max(jnp.max(top, axis=0, keepdims=True), axis=1, keepdims=True))
+        bound = jnp.maximum(tops[0] * tops[1] * MARGIN, 2.0**-90)
+        scale = 1.0 / (n_energy * bound)
+        bound_out[...] = jnp.broadcast_to(bound, (1, 128))
+
         for s in range(8):
             hats = []
             for part, sign in ((0, 1), (1, -1)):
@@ -246,13 +254,20 @@
             @pl.when(dest != me)
             def _():
                 pltpu.make_async_remote_copy(
-                    code.at[dest], o_ref.at[unit_here], psend.at[dest], precv.at[unit_here],
+                    bound_out, bound_in.at[unit_here], bsend.at[dest], brecv.at[unit_here],
                     device_id=(space, dest), device_id_type=MESH,
                 ).start()
+                pltpu.make_async_remote_copy(
+                    code.at[dest], back.at[unit_here], psend.at[dest], precv.at[unit_here],
+                    device_id=(space, dest), device_id_type=MESH,
+                ).start()
 
             @pl.when(dest == me)
             def _():
-                pltpu.make_async_copy(code.at[dest], o_ref.at[unit_here], precv.at[unit_here]).start()
+                pltpu.make_async_copy(
+                    bound_out, bound_in.at[unit_here], brecv.at[unit_here]
+                ).start()
+                pltpu.make_async_copy(code.at[dest], back.at[unit_here], precv.at[unit_here]).start()
 
         @pl.loop(0, 32)
         def _(k):
@@ -260,7 +275,11 @@
 
     @pl.loop(0, 24)
     def _(k):
-        pltpu.make_async_copy(o_ref.at[k], o_ref.at[k], precv.at[k]).wait()
+        t, rows = unit_rows(k)
+        pltpu.make_async_copy(bound_in.at[k], bound_in.at[k], brecv.at[k]).wait()
+        pltpu.make_async_copy(back.at[k], back.at[k], precv.at[k]).wait()
+        bound = jnp.concatenate([bound_in[k], bound_in[k]], axis=1)
+        o_ref[0, 0, t, rows, :] = decode(back[k].astype(F32), bound)
 
     for copy in halos:
         copy.wait_send()
@@ -281,14 +300,15 @@
         def _(k):
             dest = lax.rem(me + k, n_energy)
             pltpu.make_async_copy(code.at[dest], code.at[dest], psend.at[dest]).wait()
+            pltpu.make_async_copy(bound_out, bound_out, bsend.at[dest]).wait()
 
 
 def on_device(n_space, n_energy, lesser, greater):
     unit = (16, 256)
     dma = pltpu.SemaphoreType.DMA
-    codes = pl.pallas_call(
+    return pl.pallas_call(
         functools.partial(kernel, n_space, n_energy),
-        out_shape=pltpu.VMEM((24, *unit), jnp.bfloat16),
+        out_shape=pltpu.VMEM(lesser.shape, F32),
         in_specs=[pl.BlockSpec(memory_space=pltpu.HBM)] * 2,
         out_specs=pl.BlockSpec(memory_space=pltpu.VMEM),
         scratch_shapes=[
@@ -300,6 +320,9 @@
             pltpu.VMEM((2, n_energy, *unit), F32),
             pltpu.VMEM((n_energy, *unit), F32),
             pltpu.VMEM((n_energy, *unit), jnp.bfloat16),
+            pltpu.VMEM((24, *unit), jnp.bfloat16),
+            pltpu.VMEM((1, 128), F32),
+            pltpu.VMEM((24, 1, 128), F32),
             dma((2,)),
             dma((2,)),
             dma((2,)),
@@ -309,14 +332,15 @@
             dma,
             dma((n_energy,)),
             dma((24,)),
-            pltpu.SemaphoreType.REGULAR((9,)),
-            pltpu.SemaphoreType.REGULAR((9,)),
+            dma((n_energy,)),
+            dma((24,)),
+            pltpu.SemaphoreType.REGULAR((2,)),
+            pltpu.SemaphoreType.REGULAR((2,)),
         ],
         compiler_params=pltpu.CompilerParams(
             collective_id=0, has_side_effects=True, vmem_limit_bytes=62 << 20
         ),
     )(lesser, greater)
-    return decode(codes.reshape(lesser.shape).astype(F32), BOUND)
 
 
 def solution(mesh):

time: 46.4 us -> 47.1 us (1.015)
  Pallas kernels: 45.1 us -> 46.3 us
  other arithmetic: 1.1 us -> 0 us
  local copies, waits for them, and re-layouts: 0 us -> 0.75 us
    pallas_call x1, Pallas kernels: 45.1 us -> 46.3 us  [on_device(): pl.pallas_call(functools.partial(kernel, n_space, n_energy), out_shape=pl...]
    select_n x2 -> x0, other arithmetic: 1.03 us -> none  [the longest x1 0.8 us: decode(): return jnp.where(code < 0, -value, value)]
    unnamed x0 -> x1, local copies, waits for them, and re-layouts: none -> 0.75 us
where the time goes in v4:
time: 47.1 us; the launch traced here: 47 us
  Pallas kernels  46.3 us (98%)
  local copies, waits for them, and re-layouts  0.75 us (2%)
    pallas_call x1, Pallas kernels, on_device(): pl.pallas_call(functools.partial(kernel, n_space, n_energy), out_shape=pl...  46.3 us

profile of v4, /device:TPU:56, one launch (start us, length us, event | category | flops | bytes accessed | tf_op | source)
XLA Modules:
  0.0 47.0 jit_solution(10099002017518088144)
XLA Ops:
  0.0 46.3 %shard_map.28 = f32[1,1,3,128,256]{4,3,2,1,0:T(8,128)S(1)} custom-call(bf16[1,1,3,128,256]{4,3,2,1,0:T(8,128)(2,1)} %l_ref.1, bf16[1,1,3,128,256]{4,3,2,1,0:T(8,128)(2,1)} %g_ref.1), custom_call_target="tpu_custom_call" | custom-call | tf_op jit(solution)/shard_map/pallas_call | solution.py:309
  46.3 0.7 %copy.4 = f32[1,1,3,128,256]{4,3,2,1,0:T(8,128)} copy(f32[1,1,3,128,256]{4,3,2,1,0:T(8,128)S(1)} %shard_map.28) | data formatting | bytes 786432

commit v5 on v4

--- a/solution.py
+++ b/solution.py
@@ -269,8 +269,17 @@
                 ).start()
                 pltpu.make_async_copy(code.at[dest], back.at[unit_here], precv.at[unit_here]).start()
 
+        def given(dest):
+            @pl.when(dest != me)
+            def _():
+                pltpu.make_async_copy(code.at[dest], code.at[dest], psend.at[dest]).wait()
+
         @pl.loop(0, 32)
         def _(k):
+            @pl.when(jnp.logical_and(core == 1, k >= 12))
+            def _():
+                given(k - 12)
+
             give(k)
 
     @pl.loop(0, 24)
@@ -299,7 +308,10 @@
         @pl.loop(1, n_energy)
         def _(k):
             dest = lax.rem(me + k, n_energy)
-            pltpu.make_async_copy(code.at[dest], code.at[dest], psend.at[dest]).wait()
+            @pl.when(jnp.logical_or(core == 0, dest >= 20))
+            def _():
+                pltpu.make_async_copy(code.at[dest], code.at[dest], psend.at[dest]).wait()
+
             pltpu.make_async_copy(bound_out, bound_out, bsend.at[dest]).wait()
 
 

time: 47.1 us -> 47 us (level)
  no operation moved by 1% of the time
where the time goes in v5:
time: 47 us; the launch traced here: 46.9 us
  Pallas kernels  46.2 us (98%)
  local copies, waits for them, and re-layouts  0.75 us (2%)
    pallas_call x1, Pallas kernels, on_device(): pl.pallas_call(functools.partial(kernel, n_space, n_energy), out_shape=pl...  46.2 us

profile of v5, /device:TPU:56, one launch (start us, length us, event | category | flops | bytes accessed | tf_op | source)
XLA Modules:
  0.0 46.9 jit_solution(13746664160784064187)
XLA Ops:
  0.0 46.2 %shard_map.28 = f32[1,1,3,128,256]{4,3,2,1,0:T(8,128)S(1)} custom-call(bf16[1,1,3,128,256]{4,3,2,1,0:T(8,128)(2,1)} %l_ref.1, bf16[1,1,3,128,256]{4,3,2,1,0:T(8,128)(2,1)} %g_ref.1), custom_call_target="tpu_custom_call" | custom-call | tf_op jit(solution)/shard_map/pallas_call | solution.py:321
  46.2 0.7 %copy.4 = f32[1,1,3,128,256]{4,3,2,1,0:T(8,128)} copy(f32[1,1,3,128,256]{4,3,2,1,0:T(8,128)S(1)} %shard_map.28) | data formatting | bytes 786432
